TPU v7x, 32 devices: a whole 2x2x4 slice. The times are simulated.
32 devices in a mesh: dp: 8 (over z, core), tensor: 4 (over y, x).
Axes of the slice: x: 2, y: 2, z: 4, core: 2. Of those that a mesh axis runs over, the one named last changes fastest.
Arguments:
- hidden: bfloat16 [1024, 18432], P('dp', 'tensor'), may hold values from -66 to 66
- grad_out: bfloat16 [1024, 4608], P('dp'), may hold values from -192 to 192
- seg_ids: int32 [1024], replicated, may hold values from 0 to 7, as said below
- seg_counts: int32 [64], P('dp'), may hold values from 1 to 31, as said below
- added_noise: bfloat16 [4608, 18432], P('dp', 'tensor'), may hold values from -6 to 6
Outputs:
- weight_grad: bfloat16 [4608, 18432], P('dp', 'tensor')
- example_norms: float32 [64], P('dp')
Inputs may be any that keep to these rules, and one draw needn't show every extreme that they name: `seg_ids`: within each sequence the ids never fall and every one of the 8 ids occurs. seg_counts[j * 8 + i] is the number of tokens of sequence j whose id is i; the counts of a sequence sum to 128.
All inputs are finite; a program needn't handle non-finite values.
Results may differ from a plain program's by a relative error of at most 0.012.
Values may be sent and summed in bfloat16 or wider, within the bound.
A program may use at most 64 MiB of HBM per device.

v0:
```python
import jax
import jax.numpy as jnp
from jax import lax
from jax.sharding import PartitionSpec as P

D = 4608
FFW = 18432
SEQ = 128
NSEG = 8


EPSILON = 1e-06
CLIP_FRACTION = 4.2


def clip_bound():
    return CLIP_FRACTION * (FFW * D * NSEG / SEQ) ** 0.5


def per_device(hidden, grad_out, seg_ids, seg_counts, added_noise):
    seq_len = hidden.shape[0]
    seg_total = seg_counts.shape[0]
    group_index = lax.axis_index("dp")
    own_segments = lax.dynamic_slice_in_dim(seg_ids, group_index * seq_len, seq_len)
    member = (own_segments[:, None] == jnp.arange(seg_total, dtype=jnp.int32)[None, :]).astype(
        jnp.float32
    )
    tok_count = jnp.dot(member, seg_counts.astype(jnp.float32), precision=lax.Precision.HIGHEST)
    scaled_local = (grad_out.astype(jnp.float32) / tok_count[:, None]).astype(jnp.bfloat16)
    gram_scaled = lax.dot_general(
        scaled_local, scaled_local, (((1,), (1,)), ((), ())), preferred_element_type=jnp.float32
    )
    gram_hidden = lax.dot_general(
        hidden, hidden, (((1,), (1,)), ((), ())), preferred_element_type=jnp.float32
    )
    partial_sq = jnp.sum(
        member * jnp.dot(gram_hidden * gram_scaled, member, precision=lax.Precision.HIGHEST), axis=0
    )
    group_sq = lax.psum(partial_sq, "tensor")
    own_norm = jnp.sqrt(group_sq + EPSILON)
    own_factor = jnp.minimum(1.0, clip_bound() / own_norm)
    tok_factor = jnp.dot(member, own_factor, precision=lax.Precision.HIGHEST)
    weighted_rows = (scaled_local.astype(jnp.float32) * tok_factor[:, None]).astype(jnp.bfloat16)
    weighted = lax.all_to_all(weighted_rows, "dp", split_axis=1, concat_axis=0, tiled=True)
    summed = lax.dot_general(
        weighted,
        lax.all_gather(hidden, "dp", axis=0, tiled=True),
        (((0,), (0,)), ((), ())),
        preferred_element_type=jnp.float32,
    )
    weight_grad = (summed + added_noise.astype(jnp.float32)).astype(jnp.bfloat16)
    return (weight_grad, own_norm)


def solution(mesh):
    placed = (P("dp", "tensor"), P("dp", None), P(), P("dp"), P("dp", "tensor"))
    return jax.shard_map(
        per_device,
        mesh=mesh,
        in_specs=placed,
        out_specs=(P("dp", "tensor"), P("dp")),
        check_vma=False,
    )
```

profile of v0, /device:TPU:1, one launch (start us, length us, event | category | flops | bytes accessed | tf_op | source)
XLA Modules:
  0.0 146.5 jit_solution(17354052769478979549)
XLA Ops:
  7.2 0.0 copy-start.1
  7.2 0.0 all-gather.2.cloned.1.call-start
  7.2 0.7 all-gather.2.cloned.1.call-update
  7.9 0.5 copy-done.1
  8.4 0.0 copy-start.2
  8.4 0.0 copy-start
  8.4 0.7 copy.7
  9.2 0.8 dynamic_slice.3
  9.9 0.0 copy-done.2
  9.9 0.1 convolution_bitcast_fusion.1
  10.1 0.0 copy-done
  10.1 0.5 fusion.11
  10.5 0.5 convolution_multiply_fusion
  11.1 0.3 fusion.2
  11.4 8.7 %psum.7 = f32[8]{0:T(128)S(1)} all-reduce(f32[8]{0:T(128)S(1)} %fusion.2), channel_id=1, replica_groups=mesh['dp'=8,'tensor'=4] {'tensor'}, use_global_device_ids=true, to_apply=%region_1.0 | all-reduce | flops 8 | bytes 64 | tf_op jit(solution)/shard_map/psum | solution.py:39
  20.1 0.0 copy-start.3
  20.1 0.1 convolution_bitcast_fusion
  20.2 0.3 multiply_convert_fusion
  20.6 0.1 copy-done.3
  20.6 68.0 %all_to_all.19 = bf16[128,8,576]{0,2,1:T(8,128)(2,1)S(1)} all-to-all(bf16[128,8,576]{0,2,1:T(8,128)(2,1)S(1)} %bitcast.23), channel_id=1, replica_groups=mesh['dp'=8,'tensor'=4] {'dp'}, dimensions={1} | all-to-all | bytes 2359296 | tf_op jit(solution)/shard_map/all_to_all | solution.py:44
  88.6 39.2 %all-gather.2.cloned.1.call-done = bf16[1024,4608]{1,0:T(8,128)(2,1)} async-done(((bf16[128,4608]{1,0:T(8,128)(2,1)}), bf16[1024,4608]{1,0:T(8,128)(2,1)}) %all-gather.2.cloned.1.call-update) | async-done | bytes 9437200 | tf_op jit(solution)/shard_map/all_gather | solution.py:47
  127.8 11.8 %add_convert_fusion = bf16[576,4608]{1,0:T(8,128)(2,1)} fusion(bf16[576,4608]{1,0:T(8,128)(2,1)} %param.9, bf16[1024,4608]{1,0:T(8,128)(2,1)} %all-gather.2.cloned.1.call-done, bf16[128,8,576]{0,2,1:T(8,128)(2,1)S(1)} %all_to_all.19), kind=kOutput, calls=%fused_computation | convolution fusion | flops 5443780608 | bytes 21233664 | tf_op jit(solution)/shard_map/dot_general | solution.py:45
  (1 shorter events, 0.0 us)
Async XLA Ops:
  7.2 1.3 copy-start.1
  7.2 120.7 %all-gather.2.cloned.1.call-start = ((), (), s32[]{:S(2)}) async-start(), calls=%async_computation.1 | async-start | bytes 10616832 | tf_op jit(solution)/shard_map/all_gather | solution.py:47
  8.4 1.5 %copy-start.2 = (s32[8]{0:T(128)S(1)}, s32[8]{0:T(128)}, u32[]{:S(2)}) copy-start(s32[8]{0:T(128)} %param.8) | copy-start | bytes 100
  8.4 1.6 %copy-start = (bf16[128,4608]{1,0:T(8,128)(2,1)S(1)}, bf16[128,4608]{1,0:T(8,128)(2,1)}, u32[]{:S(2)}) copy-start(bf16[128,4608]{1,0:T(8,128)(2,1)} %param.5) | copy-start | bytes 3538948
  20.1 0.5 copy-start.3
Sparse Core Ops, SparseCore 0:
  9.6 118.1 all-gather.1
where the time goes:
time: 147 us
  blocking collectives  76.7 us (52%)
  waiting for transfers between devices  39.9 us (27%)
  between operations  14.1 us (10%)
  matrix products  13.4 us (9%)
  local copies, waits for them, and re-layouts  2.08 us (1%)
    all_to_all x1, blocking collectives, per_device(): lax.all_to_all(weighted_rows, 'dp', split_axis=1, concat_axis=0, tiled=True)  68 us
    all_gather x1, waiting for transfers between devices, per_device(): lax.all_gather(hidden, 'dp', axis=0, tiled=True)  39.2 us
    dot_general x1, matrix products, per_device(): lax.dot_general(weighted, lax.all_gather(hidden, 'dp', axis=0, tiled=True...  11.8 us
    psum x1, blocking collectives, per_device(): group_sq = lax.psum(partial_sq, 'tensor')  8.73 us
  transfers between devices with their start and end apart: 1, of which 1 were waited for; matrix products, arithmetic and copies ran while one was open for 2% of the time, Pallas kernels for 0%

commit v1 on v0

v1 whole, which is shorter than its diff:
```python
import functools
import math

import jax
import jax.numpy as jnp
from jax import lax
from jax.experimental import pallas as pl
from jax.experimental.pallas import tpu as pltpu
from jax.sharding import PartitionSpec as P

D = 4608
FFW = 18432
SEQ = 128
NSEG = 8
CORES = 2

EPSILON = 1e-06
CLIP_FRACTION = 4.2
MESH = pl.DeviceIdType.MESH
EARLY = 2


def clip_bound():
    return CLIP_FRACTION * (FFW * D * NSEG / SEQ) ** 0.5


def rows_of(index, count):
    return pl.ds(pl.multiple_of(index * count, count), count)


def kernel(
    ndp, nt, width, share, ids_ref, hid_ref, grad_ref, noise_ref, out_ref, norms_ref,
    hall, g, gt, gt_in, wt, buf, sq_t, sq_d,
    load_sem, own_send, fwd_send, mate_send, hid_recv, gt_send, gt_recv,
    share_send, share_recv, sqt_send, sqt_recv, sqd_send, sqd_recv, out_sem,
):
    d = lax.axis_index("dp")
    t = lax.axis_index("tensor")
    nz = ndp // CORES
    z = lax.div(d, CORES)
    c = lax.rem(d, CORES)
    mate = d + 1 - 2 * c
    rows, cols = buf.shape
    nk = cols // width
    part = rows // share

    def remote(src, dst, send, recv, device):
        return pltpu.make_async_remote_copy(
            src_ref=src, dst_ref=dst, send_sem=send, recv_sem=recv, device_id=device, device_id_type=MESH
        )

    def others(count, me, body):
        def step(i, carry):
            body(lax.rem(me + i, count))
            return carry

        lax.fori_loop(1, count, step, 0)

    def repeat(low, high, body):
        def step(i, carry):
            body(i)
            return carry

        lax.fori_loop(low, high, step, 0)

    load_h = pltpu.make_async_copy(hid_ref, hall.at[rows_of(d, SEQ), :], load_sem.at[0])
    load_g = pltpu.make_async_copy(grad_ref, g, load_sem.at[1])
    load_n = pltpu.make_async_copy(noise_ref, buf, load_sem.at[2])
    load_h.start()
    load_g.start()

    barrier = pltpu.get_barrier_semaphore()
    others(ndp, d, lambda j: pl.semaphore_signal(barrier, inc=1, device_id={"dp": j}, device_id_type=MESH))
    others(nt, t, lambda m: pl.semaphore_signal(barrier, inc=1, device_id={"tensor": m}, device_id_type=MESH))
    load_h.wait()
    pl.semaphore_wait(barrier, ndp + nt - 2)

    def chunk(j, k):
        return hall.at[rows_of(j, SEQ), rows_of(k, width)]

    def to(j, k, send, device):
        return remote(chunk(j, k), chunk(j, k), send, hid_recv.at[j, k], {"dp": device})

    def send_own(k):
        @pl.when(z + 1 < nz)
        def _():
            to(d, k, own_send.at[0], d + CORES).start()

        @pl.when(z > 0)
        def _():
            to(d, k, own_send.at[1], d - CORES).start()

        to(d, k, mate_send.at[z], mate).start()

    repeat(0, EARLY, send_own)

    load_g.wait()

    def turn(i):
        gt[rows_of(i, SEQ), :] = g[:, rows_of(i, SEQ)].T

    repeat(0, D // SEQ, turn)
    piece = (t if share > 1 else 0) * part

    def gt_copy(j, src_seq):
        return remote(
            gt.at[pl.ds(pl.multiple_of(j * rows + piece, 16), part), :],
            gt_in.at[src_seq, pl.ds(pl.multiple_of(piece, 16), part), :],
            gt_send.at[j], gt_recv.at[src_seq], {"dp": j},
        )

    others(ndp, d, lambda j: gt_copy(j, d).start())
    gt_in[d, pl.ds(pl.multiple_of(piece, 16), part), :] = gt[pl.ds(pl.multiple_of(d * rows + piece, 16), part), :]
    repeat(EARLY, nk, send_own)
    load_n.start()

    def members(j):
        ids = ids_ref[pl.ds(j, 1), :]
        inside = (lax.broadcasted_iota(jnp.int32, (NSEG, SEQ), 0) == ids).astype(jnp.float32)
        return ids, inside, jnp.sum(inside, axis=1, keepdims=True)

    ids, inside, count = members(d)
    contract = (((1,), (1,)), ((), ()))
    own = hall[rows_of(d, SEQ), :]
    gram_hidden = lax.dot_general(own, own, contract, preferred_element_type=jnp.float32)
    gram_raw = lax.dot_general(g[...], g[...], contract, preferred_element_type=jnp.float32)
    wide = jnp.broadcast_to(ids.astype(jnp.float32), (SEQ, SEQ))
    pairs = jnp.where(wide == wide.T, gram_hidden * gram_raw, 0.0)
    per_token = jnp.sum(pairs, axis=0, keepdims=True)
    partial = jnp.sum(inside * per_token, axis=1, keepdims=True)
    sq_t[t] = jnp.broadcast_to(partial, (NSEG, SEQ))

    def sqt_copy(m, src):
        return remote(sq_t.at[src], sq_t.at[src], sqt_send.at[m], sqt_recv.at[src], {"tensor": m})

    others(nt, t, lambda m: sqt_copy(m, t).start())
    others(nt, t, lambda m: sqt_copy(m, m).wait_recv())
    total = sq_t[0]
    for m in range(1, nt):
        total = total + sq_t[m]
    total = total / (count * count)
    sq_d[d] = total
    norms_ref[...] = jnp.sqrt(total + EPSILON)

    def sqd_copy(j, src):
        return remote(sq_d.at[src], sq_d.at[src], sqd_send.at[j], sqd_recv.at[src], {"dp": j})

    others(ndp, d, lambda j: sqd_copy(j, d).start())

    def forward(h, k):
        for way in (1, -1):
            far = z + way * h
            ahead = z - way

            @pl.when((far >= 0) & (far < nz))
            def _():
                j = far * CORES + c
                to(j, k, mate_send.at[far], mate).wait_recv()

                @pl.when((ahead >= 0) & (ahead < nz))
                def _():
                    to(j, k, fwd_send.at[far], ahead * CORES + c).start()

                to(j, k, mate_send.at[far], mate).start()

    repeat(0, nk, lambda k: forward(1, k))

    others(ndp, d, lambda j: gt_copy(j, j).wait_recv())

    def share_copy(m, src):
        block = gt_in.at[:, pl.ds(pl.multiple_of(src * part, 16), part), :]
        return remote(block, block, share_send.at[m], share_recv.at[src], {"tensor": m})

    if share > 1:
        others(nt, t, lambda m: share_copy(m, t).start())
    repeat(nk, nk * (nz - 2), lambda i: forward(1 + lax.div(i, nk), lax.rem(i, nk)))
    if share > 1:
        others(nt, t, lambda m: share_copy(m, m).wait_recv())
    others(ndp, d, lambda j: sqd_copy(j, j).wait_recv())

    def weigh(j):
        _, inside, count = members(j)
        norm = jnp.sqrt(sq_d[j] + EPSILON)
        factor = jnp.minimum(1.0, clip_bound() / norm)
        tok_count = jnp.sum(inside * count, axis=0, keepdims=True)
        tok_factor = jnp.sum(inside * factor, axis=0, keepdims=True)
        scaled = (gt_in[j].astype(jnp.float32) / tok_count).astype(jnp.bfloat16)
        wt[:, rows_of(j, SEQ)] = (scaled.astype(jnp.float32) * tok_factor).astype(jnp.bfloat16)

    repeat(0, ndp, weigh)
    load_n.wait()

    def out_copy(k):
        return pltpu.make_async_copy(
            buf.at[:, rows_of(k, width)], out_ref.at[:, rows_of(k, width)], out_sem.at[k]
        )

    def multiply(k):
        repeat(0, nz, lambda far: to(far * CORES + 1 - c, k, mate_send.at[far], mate).wait_recv())
        at = rows_of(k, width)
        summed = jnp.dot(wt[...], hall[:, at], preferred_element_type=jnp.float32)
        buf[:, at] = (summed + buf[:, at].astype(jnp.float32)).astype(jnp.bfloat16)
        out_copy(k).start()

    def last(k):
        @pl.when(k < nk)
        def _():
            forward(nz - 1, k)

        @pl.when(k > 0)
        def _():
            multiply(k - 1)

    repeat(0, nk + 1, last)

    def sent(far, sem):
        block = hall.at[rows_of(far * CORES + c, SEQ), :]
        remote(block, block, sem, hid_recv.at[0, 0], {"dp": mate}).wait_send()

    @pl.when(z + 1 < nz)
    def _():
        sent(z, own_send.at[0])

    @pl.when(z > 0)
    def _():
        sent(z, own_send.at[1])

    repeat(0, nz, lambda far: sent(far, mate_send.at[far]))

    def sent_on(far):
        inner = (z > 0) & (z < nz - 1) & (far != z)

        @pl.when(inner)
        def _():
            sent(far, fwd_send.at[far])

    repeat(0, nz, sent_on)
    others(ndp, d, lambda j: gt_copy(j, d).wait_send())
    others(ndp, d, lambda j: sqd_copy(j, d).wait_send())
    others(nt, t, lambda m: sqt_copy(m, t).wait_send())
    if share > 1:
        others(nt, t, lambda m: share_copy(m, t).wait_send())
    repeat(0, nk, lambda k: out_copy(k).wait())


def per_device(ndp, nt, hidden, grad_out, seg_ids, seg_counts, added_noise):
    rows, cols = added_noise.shape
    width = next(w for w in (512, 384, 256, 128) if cols % w == 0)
    share = nt if rows % (16 * nt) == 0 else 1
    nz = ndp // CORES
    nk = cols // width
    dma = pltpu.SemaphoreType.DMA
    anywhere = pl.BlockSpec(memory_space=pl.ANY)
    vmem = pl.BlockSpec(memory_space=pltpu.VMEM)
    out, norms = pl.pallas_call(
        functools.partial(kernel, ndp, nt, width, share),
        out_shape=(
            jax.ShapeDtypeStruct((rows, cols), jnp.bfloat16),
            jax.ShapeDtypeStruct((NSEG, SEQ), jnp.float32),
        ),
        in_specs=[vmem, anywhere, anywhere, anywhere],
        out_specs=(anywhere, vmem),
        scratch_shapes=[
            pltpu.VMEM((ndp * SEQ, cols), jnp.bfloat16),
            pltpu.VMEM((SEQ, D), jnp.bfloat16),
            pltpu.VMEM((D, SEQ), jnp.bfloat16),
            pltpu.VMEM((ndp, rows, SEQ), jnp.bfloat16),
            pltpu.VMEM((rows, ndp * SEQ), jnp.bfloat16),
            pltpu.VMEM((rows, cols), jnp.bfloat16),
            pltpu.VMEM((nt, NSEG, SEQ), jnp.float32),
            pltpu.VMEM((ndp, NSEG, SEQ), jnp.float32),
            dma((3,)), dma((2,)), dma((nz,)), dma((nz,)), dma((ndp, nk)), dma((ndp,)), dma((ndp,)),
            dma((nt,)), dma((nt,)), dma((nt,)), dma((nt,)), dma((ndp,)), dma((ndp,)), dma((nk,)),
        ],
        compiler_params=pltpu.CompilerParams(
            collective_id=0, has_side_effects=True, vmem_limit_bytes=48 * 1024 * 1024
        ),
        cost_estimate=pl.CostEstimate(
            flops=2 * ndp * SEQ * rows * cols, bytes_accessed=4 * rows * cols, transcendentals=0
        ),
    )(seg_ids.reshape(ndp, SEQ), hidden, grad_out, added_noise)
    return out, norms[:, 0]


def solution(mesh):
    placed = (P("dp", "tensor"), P("dp", None), P(), P("dp"), P("dp", "tensor"))
    return jax.shard_map(
        functools.partial(per_device, mesh.shape["dp"], mesh.shape["tensor"]),
        mesh=mesh,
        in_specs=placed,
        out_specs=(P("dp", "tensor"), P("dp")),
        check_vma=False,
    )
```

time: 147 us -> 102 us (0.69)
  Pallas kernels: 0 us -> 92.1 us
  blocking collectives: 76.7 us -> 0 us
  waiting for transfers between devices: 39.9 us -> 0 us
  between operations: 14.1 us -> 0.65 us
  matrix products: 13.4 us -> 0 us
  local copies, waits for them, and re-layouts: 2.08 us -> 9.07 us
    pallas_call x0 -> x1, Pallas kernels: none -> 92.1 us  [per_device(): pl.pallas_call(functools.partial(kernel, ndp, nt, width, share), out_shap...]
    all_to_all x1 -> x0, blocking collectives: 68 us -> none  [per_device(): lax.all_to_all(weighted_rows, 'dp', split_axis=1, concat_axis=0, tiled=True)]
    all_gather x1 -> x0, waiting for transfers between devices: 39.2 us -> none  [per_device(): lax.all_gather(hidden, 'dp', axis=0, tiled=True)]
    dot_general x6 -> x0, matrix products: 13.4 us -> none  [the longest x1 11.8 us: per_device(): lax.dot_general(weighted, lax.all_gather(hidden, 'dp', axis=0, tiled=True...]
    psum x1 -> x0, blocking collectives: 8.73 us -> none  [per_device(): group_sq = lax.psum(partial_sq, 'tensor')]
    unnamed x9 -> x7, local copies, waits for them, and re-layouts: 1.31 us -> 8.44 us
  transfers between devices with their start and end apart: 1 -> 0, of which waited for: 1 -> 0; matrix products, arithmetic and copies ran while one was open for 2% -> 0% of each run, Pallas kernels for 0% -> 0%
where the time goes in v1:
time: 102 us
  Pallas kernels  92.1 us (90%)
  local copies, waits for them, and re-layouts  9.07 us (9%)
    pallas_call x1, Pallas kernels, per_device(): pl.pallas_call(functools.partial(kernel, ndp, nt, width, share), out_shap...  92.1 us
    unnamed x7, local copies, waits for them, and re-layouts  8.44 us

profile of v1, /device:TPU:1, one launch (start us, length us, event | category | flops | bytes accessed | tf_op | source)
XLA Modules:
  0.0 101.8 jit_solution(18238961984582131891)
XLA Ops:
  0.6 0.0 copy-start
  0.6 1.3 %copy-done = bf16[128,4608]{1,0:T(8,128)(2,1)S(1)} copy-done((bf16[128,4608]{1,0:T(8,128)(2,1)S(1)}, bf16[128,4608]{1,0:T(8,128)(2,1)}, u32[]{:S(2)}) %copy-start) | copy-done | bytes 1179672
  1.9 0.0 copy-start.1
  1.9 1.3 %copy-done.1 = bf16[128,4608]{1,0:T(8,128)(2,1)S(1)} copy-done((bf16[128,4608]{1,0:T(8,128)(2,1)S(1)}, bf16[128,4608]{1,0:T(8,128)(2,1)}, u32[]{:S(2)}) %copy-start.1) | copy-done | bytes 1179672
  3.2 0.0 copy-start.2
  3.2 0.7 copy-done.2
  3.9 92.1 %shard_map.59 = (bf16[576,4608]{1,0:T(8,128)(2,1)}, f32[8,128]{1,0:T(8,128)S(1)}) custom-call(s32[8,128]{1,0:T(8,128)S(1)} %bitcast.1, bf16[128,4608]{1,0:T(8,128)(2,1)S(1)} %copy-done, bf16[128,4608]{1,0:T(8,128)(2,1)S(1)} %copy-done.1, bf16[576,4608]{1,0:T(8,128)(2,1)} %noise_ref.1), custom_call_target="tpu_custom_call" | custom-call | flops 5435817984 | bytes 10616832 | tf_op jit(solution)/shard_map/pallas_call | solution.py:255
  95.9 0.6 slice_reduce_fusion
  96.6 5.2 %copy.7 = bf16[576,4608]{1,0:T(8,128)(2,1)} copy(bf16[576,4608]{1,0:T(8,128)(2,1)} %get-tuple-element.8) | data formatting | bytes 10616832
Async XLA Ops:
  0.6 1.3 %copy-start = (bf16[128,4608]{1,0:T(8,128)(2,1)S(1)}, bf16[128,4608]{1,0:T(8,128)(2,1)}, u32[]{:S(2)}) copy-start(bf16[128,4608]{1,0:T(8,128)(2,1)} %hid_ref.1) | copy-start | bytes 3538948
  1.9 1.3 %copy-start.1 = (bf16[128,4608]{1,0:T(8,128)(2,1)S(1)}, bf16[128,4608]{1,0:T(8,128)(2,1)}, u32[]{:S(2)}) copy-start(bf16[128,4608]{1,0:T(8,128)(2,1)} %grad_ref.1) | copy-start | bytes 3538948
  3.2 0.7 copy-start.2

commit v2 on v1

--- a/solution.py
+++ b/solution.py
@@ -17,7 +17,7 @@
 EPSILON = 1e-06
 CLIP_FRACTION = 4.2
 MESH = pl.DeviceIdType.MESH
-EARLY = 2
+EARLY = 3
 
 
 def clip_bound():
@@ -29,10 +29,10 @@
 
 
 def kernel(
-    ndp, nt, width, share, ids_ref, hid_ref, grad_ref, noise_ref, out_ref, norms_ref,
-    hall, g, gt, gt_in, wt, buf, sq_t, sq_d,
+    ndp, nt, width, share, ids_in, hid_ref, grad_ref, noise_ref, out_ref, norms_ref,
+    ids_ref, hall, g, gt, gt_in, wt, sq_t, sq_d,
     load_sem, own_send, fwd_send, mate_send, hid_recv, gt_send, gt_recv,
-    share_send, share_recv, sqt_send, sqt_recv, sqd_send, sqd_recv, out_sem,
+    share_send, share_recv, sqt_send, sqt_recv, sqd_send, sqd_recv,
 ):
     d = lax.axis_index("dp")
     t = lax.axis_index("tensor")
@@ -40,7 +40,7 @@
     z = lax.div(d, CORES)
     c = lax.rem(d, CORES)
     mate = d + 1 - 2 * c
-    rows, cols = buf.shape
+    rows, cols = out_ref.shape
     nk = cols // width
     part = rows // share
 
@@ -65,9 +65,11 @@
 
     load_h = pltpu.make_async_copy(hid_ref, hall.at[rows_of(d, SEQ), :], load_sem.at[0])
     load_g = pltpu.make_async_copy(grad_ref, g, load_sem.at[1])
-    load_n = pltpu.make_async_copy(noise_ref, buf, load_sem.at[2])
+    load_n = pltpu.make_async_copy(noise_ref, out_ref, load_sem.at[2])
+    load_i = pltpu.make_async_copy(ids_in, ids_ref, load_sem.at[3])
     load_h.start()
     load_g.start()
+    load_i.start()
 
     barrier = pltpu.get_barrier_semaphore()
     others(ndp, d, lambda j: pl.semaphore_signal(barrier, inc=1, device_id={"dp": j}, device_id_type=MESH))
@@ -119,6 +121,7 @@
         inside = (lax.broadcasted_iota(jnp.int32, (NSEG, SEQ), 0) == ids).astype(jnp.float32)
         return ids, inside, jnp.sum(inside, axis=1, keepdims=True)
 
+    load_i.wait()
     ids, inside, count = members(d)
     contract = (((1,), (1,)), ((), ()))
     own = hall[rows_of(d, SEQ), :]
@@ -140,7 +143,7 @@
         total = total + sq_t[m]
     total = total / (count * count)
     sq_d[d] = total
-    norms_ref[...] = jnp.sqrt(total + EPSILON)
+    norms_ref[...] = jnp.sqrt(total + EPSILON)[:, 0]
 
     def sqd_copy(j, src):
         return remote(sq_d.at[src], sq_d.at[src], sqd_send.at[j], sqd_recv.at[src], {"dp": j})
@@ -187,32 +190,6 @@
         scaled = (gt_in[j].astype(jnp.float32) / tok_count).astype(jnp.bfloat16)
         wt[:, rows_of(j, SEQ)] = (scaled.astype(jnp.float32) * tok_factor).astype(jnp.bfloat16)
 
-    repeat(0, ndp, weigh)
-    load_n.wait()
-
-    def out_copy(k):
-        return pltpu.make_async_copy(
-            buf.at[:, rows_of(k, width)], out_ref.at[:, rows_of(k, width)], out_sem.at[k]
-        )
-
-    def multiply(k):
-        repeat(0, nz, lambda far: to(far * CORES + 1 - c, k, mate_send.at[far], mate).wait_recv())
-        at = rows_of(k, width)
-        summed = jnp.dot(wt[...], hall[:, at], preferred_element_type=jnp.float32)
-        buf[:, at] = (summed + buf[:, at].astype(jnp.float32)).astype(jnp.bfloat16)
-        out_copy(k).start()
-
-    def last(k):
-        @pl.when(k < nk)
-        def _():
-            forward(nz - 1, k)
-
-        @pl.when(k > 0)
-        def _():
-            multiply(k - 1)
-
-    repeat(0, nk + 1, last)
-
     def sent(far, sem):
         block = hall.at[rows_of(far * CORES + c, SEQ), :]
         remote(block, block, sem, hid_recv.at[0, 0], {"dp": mate}).wait_send()
@@ -225,61 +202,86 @@
     def _():
         sent(z, own_send.at[1])
 
-    repeat(0, nz, lambda far: sent(far, mate_send.at[far]))
-
-    def sent_on(far):
-        inner = (z > 0) & (z < nz - 1) & (far != z)
-
-        @pl.when(inner)
-        def _():
-            sent(far, fwd_send.at[far])
-
-    repeat(0, nz, sent_on)
+    sent(z, mate_send.at[z])
     others(ndp, d, lambda j: gt_copy(j, d).wait_send())
     others(ndp, d, lambda j: sqd_copy(j, d).wait_send())
     others(nt, t, lambda m: sqt_copy(m, t).wait_send())
     if share > 1:
         others(nt, t, lambda m: share_copy(m, t).wait_send())
-    repeat(0, nk, lambda k: out_copy(k).wait())
+    repeat(0, ndp, weigh)
+    load_n.wait()
+
+    def multiply(k):
+        repeat(0, nz, lambda far: to(far * CORES + 1 - c, k, mate_send.at[far], mate).wait_recv())
+        at = rows_of(k, width)
+        summed = jnp.dot(wt[...], hall[:, at], preferred_element_type=jnp.float32)
+        out_ref[:, at] = (summed + out_ref[:, at].astype(jnp.float32)).astype(jnp.bfloat16)
+
+    def last(k):
+        @pl.when(k < nk)
+        def _():
+            forward(nz - 1, k)
+
+        @pl.when(k > 0)
+        def _():
+            multiply(k - 1)
+
+    repeat(0, nk + 1, last)
+
+    def sent_on(far):
+        @pl.when(far != z)
+        def _():
+            sent(far, mate_send.at[far])
+
+        @pl.when((z > 0) & (z < nz - 1) & (far != z))
+        def _():
+            sent(far, fwd_send.at[far])
+
+    repeat(0, nz, sent_on)
 
 
 def per_device(ndp, nt, hidden, grad_out, seg_ids, seg_counts, added_noise):
     rows, cols = added_noise.shape
-    width = next(w for w in (512, 384, 256, 128) if cols % w == 0)
+    width = next(w for w in (256, 384, 128) if cols % w == 0)
     share = nt if rows % (16 * nt) == 0 else 1
     nz = ndp // CORES
     nk = cols // width
     dma = pltpu.SemaphoreType.DMA
-    anywhere = pl.BlockSpec(memory_space=pl.ANY)
+    hbm = pl.BlockSpec(memory_space=pltpu.HBM)
     vmem = pl.BlockSpec(memory_space=pltpu.VMEM)
     out, norms = pl.pallas_call(
         functools.partial(kernel, ndp, nt, width, share),
         out_shape=(
             jax.ShapeDtypeStruct((rows, cols), jnp.bfloat16),
-            jax.ShapeDtypeStruct((NSEG, SEQ), jnp.float32),
+            jax.ShapeDtypeStruct((NSEG,), jnp.float32),
         ),
-        in_specs=[vmem, anywhere, anywhere, anywhere],
-        out_specs=(anywhere, vmem),
+        in_specs=[hbm] * 4,
+        out_specs=(vmem, vmem),
         scratch_shapes=[
+            pltpu.VMEM((ndp, SEQ), jnp.int32),
             pltpu.VMEM((ndp * SEQ, cols), jnp.bfloat16),
             pltpu.VMEM((SEQ, D), jnp.bfloat16),
             pltpu.VMEM((D, SEQ), jnp.bfloat16),
             pltpu.VMEM((ndp, rows, SEQ), jnp.bfloat16),
             pltpu.VMEM((rows, ndp * SEQ), jnp.bfloat16),
-            pltpu.VMEM((rows, cols), jnp.bfloat16),
             pltpu.VMEM((nt, NSEG, SEQ), jnp.float32),
             pltpu.VMEM((ndp, NSEG, SEQ), jnp.float32),
-            dma((3,)), dma((2,)), dma((nz,)), dma((nz,)), dma((ndp, nk)), dma((ndp,)), dma((ndp,)),
-            dma((nt,)), dma((nt,)), dma((nt,)), dma((nt,)), dma((ndp,)), dma((ndp,)), dma((nk,)),
+            dma((4,)), dma((2,)), dma((nz,)), dma((nz,)), dma((ndp, nk)), dma((ndp,)), dma((ndp,)),
+            dma((nt,)), dma((nt,)), dma((nt,)), dma((nt,)), dma((ndp,)), dma((ndp,)),
         ],
         compiler_params=pltpu.CompilerParams(
-            collective_id=0, has_side_effects=True, vmem_limit_bytes=48 * 1024 * 1024
+            collective_id=0, has_side_effects=True, vmem_limit_bytes=32 * 1024 * 1024
         ),
         cost_estimate=pl.CostEstimate(
             flops=2 * ndp * SEQ * rows * cols, bytes_accessed=4 * rows * cols, transcendentals=0
         ),
-    )(seg_ids.reshape(ndp, SEQ), hidden, grad_out, added_noise)
-    return out, norms[:, 0]
+    )(
+        *(
+            pltpu.with_memory_space_constraint(x, pltpu.HBM)
+            for x in (seg_ids.reshape(ndp, SEQ), hidden, grad_out, added_noise)
+        )
+    )
+    return out, norms
 
 
 def solution(mesh):

time: 102 us -> 94.6 us (0.927)
  local copies, waits for them, and re-layouts: 9.07 us -> 2.89 us
  Pallas kernels: 92.1 us -> 91 us
    unnamed x7 -> x2, local copies, waits for them, and re-layouts: 8.44 us -> 2.89 us
    pallas_call x1, Pallas kernels: 92.1 us -> 91 us  [per_device(): pl.pallas_call(functools.partial(kernel, ndp, nt, width, share), out_shap...]
where the time goes in v2:
time: 94.6 us; the launch traced here: 94.5 us
  Pallas kernels  91 us (96%)
  local copies, waits for them, and re-layouts  2.89 us (3%)
    pallas_call x1, Pallas kernels, per_device(): pl.pallas_call(functools.partial(kernel, ndp, nt, width, share), out_shap...  91 us
    unnamed x2, local copies, waits for them, and re-layouts  2.89 us

profile of v2, /device:TPU:1, one launch (start us, length us, event | category | flops | bytes accessed | tf_op | source)
XLA Modules:
  0.0 94.5 jit_solution(13383497650110956069)
XLA Ops:
  0.6 91.0 %shard_map.59 = (bf16[576,4608]{1,0:T(8,128)(2,1)S(1)}, f32[8]{0:T(128)S(1)}) custom-call(s32[8,128]{1,0:T(8,128)} %bitcast.1, bf16[128,4608]{1,0:T(8,128)(2,1)} %hid_ref.1, bf16[128,4608]{1,0:T(8,128)(2,1)} %grad_ref.1, bf16[576,4608]{1,0:T(8,128)(2,1)} %noise_ref.1), custom_call_target="tpu_custom_call" | custom-call | flops 5435817984 | bytes 10616832 | tf_op jit(solution)/shard_map/pallas_call | solution.py:252
  91.6 2.4 %copy.8 = bf16[576,4608]{1,0:T(8,128)(2,1)} copy(bf16[576,4608]{1,0:T(8,128)(2,1)S(1)} %get-tuple-element.4) | data formatting | bytes 10616832
  94.0 0.5 copy.9

commit v3 on v2

--- a/solution.py
+++ b/solution.py
@@ -31,7 +31,7 @@
 def kernel(
     ndp, nt, width, share, ids_in, hid_ref, grad_ref, noise_ref, out_ref, norms_ref,
     ids_ref, hall, g, gt, gt_in, wt, sq_t, sq_d,
-    load_sem, own_send, fwd_send, mate_send, hid_recv, gt_send, gt_recv,
+    load_sem, hid_load, own_send, fwd_send, mate_send, hid_recv, gt_send, gt_recv,
     share_send, share_recv, sqt_send, sqt_recv, sqd_send, sqd_recv,
 ):
     d = lax.axis_index("dp")
@@ -63,27 +63,32 @@
 
         lax.fori_loop(low, high, step, 0)
 
-    load_h = pltpu.make_async_copy(hid_ref, hall.at[rows_of(d, SEQ), :], load_sem.at[0])
-    load_g = pltpu.make_async_copy(grad_ref, g, load_sem.at[1])
-    load_n = pltpu.make_async_copy(noise_ref, out_ref, load_sem.at[2])
-    load_i = pltpu.make_async_copy(ids_in, ids_ref, load_sem.at[3])
-    load_h.start()
+    def load_h(k):
+        return pltpu.make_async_copy(
+            hid_ref.at[:, rows_of(k, width)], hall.at[k, rows_of(d, SEQ), :], hid_load.at[k]
+        )
+
+    load_g = pltpu.make_async_copy(grad_ref, g, load_sem.at[0])
+    load_n = pltpu.make_async_copy(noise_ref, out_ref, load_sem.at[1])
+    load_i = pltpu.make_async_copy(ids_in, ids_ref, load_sem.at[2])
+    repeat(0, nk, lambda k: load_h(k).start())
     load_g.start()
     load_i.start()
 
     barrier = pltpu.get_barrier_semaphore()
     others(ndp, d, lambda j: pl.semaphore_signal(barrier, inc=1, device_id={"dp": j}, device_id_type=MESH))
     others(nt, t, lambda m: pl.semaphore_signal(barrier, inc=1, device_id={"tensor": m}, device_id_type=MESH))
-    load_h.wait()
     pl.semaphore_wait(barrier, ndp + nt - 2)
 
     def chunk(j, k):
-        return hall.at[rows_of(j, SEQ), rows_of(k, width)]
+        return hall.at[k, rows_of(j, SEQ), :]
 
     def to(j, k, send, device):
         return remote(chunk(j, k), chunk(j, k), send, hid_recv.at[j, k], {"dp": device})
 
     def send_own(k):
+        load_h(k).wait()
+
         @pl.when(z + 1 < nz)
         def _():
             to(d, k, own_send.at[0], d + CORES).start()
@@ -124,8 +129,12 @@
     load_i.wait()
     ids, inside, count = members(d)
     contract = (((1,), (1,)), ((), ()))
-    own = hall[rows_of(d, SEQ), :]
-    gram_hidden = lax.dot_general(own, own, contract, preferred_element_type=jnp.float32)
+
+    def gram(k, held):
+        own = hall[k, rows_of(d, SEQ), :]
+        return held + lax.dot_general(own, own, contract, preferred_element_type=jnp.float32)
+
+    gram_hidden = lax.fori_loop(0, nk, gram, jnp.zeros((SEQ, SEQ), jnp.float32))
     gram_raw = lax.dot_general(g[...], g[...], contract, preferred_element_type=jnp.float32)
     wide = jnp.broadcast_to(ids.astype(jnp.float32), (SEQ, SEQ))
     pairs = jnp.where(wide == wide.T, gram_hidden * gram_raw, 0.0)
@@ -191,7 +200,7 @@
         wt[:, rows_of(j, SEQ)] = (scaled.astype(jnp.float32) * tok_factor).astype(jnp.bfloat16)
 
     def sent(far, sem):
-        block = hall.at[rows_of(far * CORES + c, SEQ), :]
+        block = hall.at[:, rows_of(far * CORES + c, SEQ), :]
         remote(block, block, sem, hid_recv.at[0, 0], {"dp": mate}).wait_send()
 
     @pl.when(z + 1 < nz)
@@ -214,7 +223,7 @@
     def multiply(k):
         repeat(0, nz, lambda far: to(far * CORES + 1 - c, k, mate_send.at[far], mate).wait_recv())
         at = rows_of(k, width)
-        summed = jnp.dot(wt[...], hall[:, at], preferred_element_type=jnp.float32)
+        summed = jnp.dot(wt[...], hall[k], preferred_element_type=jnp.float32)
         out_ref[:, at] = (summed + out_ref[:, at].astype(jnp.float32)).astype(jnp.bfloat16)
 
     def last(k):
@@ -238,6 +247,18 @@
             sent(far, fwd_send.at[far])
 
     repeat(0, nz, sent_on)
+
+
+def place(pieces, held_ref, held_norms_ref, out_ref, norms_ref, sem):
+    part = out_ref.shape[0] // pieces
+    copies = [pltpu.make_async_copy(held_norms_ref, norms_ref, sem.at[pieces])]
+    for i in range(pieces):
+        at = pl.ds(i * part, part)
+        copies.append(pltpu.make_async_copy(held_ref.at[at, :], out_ref.at[at, :], sem.at[i]))
+    for copy in copies:
+        copy.start()
+    for copy in copies:
+        copy.wait()
 
 
 def per_device(ndp, nt, hidden, grad_out, seg_ids, seg_counts, added_noise):
@@ -259,14 +280,14 @@
         out_specs=(vmem, vmem),
         scratch_shapes=[
             pltpu.VMEM((ndp, SEQ), jnp.int32),
-            pltpu.VMEM((ndp * SEQ, cols), jnp.bfloat16),
+            pltpu.VMEM((nk, ndp * SEQ, width), jnp.bfloat16),
             pltpu.VMEM((SEQ, D), jnp.bfloat16),
             pltpu.VMEM((D, SEQ), jnp.bfloat16),
             pltpu.VMEM((ndp, rows, SEQ), jnp.bfloat16),
             pltpu.VMEM((rows, ndp * SEQ), jnp.bfloat16),
             pltpu.VMEM((nt, NSEG, SEQ), jnp.float32),
             pltpu.VMEM((ndp, NSEG, SEQ), jnp.float32),
-            dma((4,)), dma((2,)), dma((nz,)), dma((nz,)), dma((ndp, nk)), dma((ndp,)), dma((ndp,)),
+            dma((3,)), dma((nk,)), dma((2,)), dma((nz,)), dma((nz,)), dma((ndp, nk)), dma((ndp,)), dma((ndp,)),
             dma((nt,)), dma((nt,)), dma((nt,)), dma((nt,)), dma((ndp,)), dma((ndp,)),
         ],
         compiler_params=pltpu.CompilerParams(
@@ -281,7 +302,19 @@
             for x in (seg_ids.reshape(ndp, SEQ), hidden, grad_out, added_noise)
         )
     )
-    return out, norms
+    pieces = 8 if rows % 128 == 0 else 9
+    return pl.pallas_call(
+        functools.partial(place, pieces),
+        out_shape=(
+            jax.ShapeDtypeStruct((rows, cols), jnp.bfloat16),
+            jax.ShapeDtypeStruct((NSEG,), jnp.float32),
+        ),
+        in_specs=[pl.BlockSpec(memory_space=pl.ANY)] * 2,
+        out_specs=(pl.BlockSpec(memory_space=pl.ANY),) * 2,
+        scratch_shapes=[dma((pieces + 1,))],
+        compiler_params=pltpu.CompilerParams(vmem_limit_bytes=1024 * 1024),
+        cost_estimate=pl.CostEstimate(flops=0, bytes_accessed=4 * rows * cols, transcendentals=0),
+    )(out, norms)
 
 
 def solution(mesh):

time: 94.6 us -> 94.5 us (level)
  local copies, waits for them, and re-layouts: 2.89 us -> 0 us
  Pallas kernels: 91 us -> 93.8 us
    unnamed x2 -> x0, local copies, waits for them, and re-layouts: 2.89 us -> none
    pallas_call x0 -> x1, Pallas kernels: none -> 2.46 us  [per_device(): pl.pallas_call(functools.partial(place, pieces), out_shape=(jax.ShapeDtyp...]
where the time goes in v3:
time: 94.5 us; the launch traced here: 94.4 us
  Pallas kernels  93.8 us (99%)
    pallas_call x1, Pallas kernels, per_device(): pl.pallas_call(functools.partial(kernel, ndp, nt, width, share), out_shap...  91.3 us
    pallas_call x1, Pallas kernels, per_device(): pl.pallas_call(functools.partial(place, pieces), out_shape=(jax.ShapeDtyp...  2.46 us

profile of v3, /device:TPU:1, one launch (start us, length us, event | category | flops | bytes accessed | tf_op | source)
XLA Modules:
  0.0 94.4 jit_solution(10307317935843216275)
XLA Ops:
  0.6 91.3 %shard_map.59 = (bf16[576,4608]{1,0:T(8,128)(2,1)S(1)}, f32[8]{0:T(128)S(1)}) custom-call(s32[8,128]{1,0:T(8,128)} %bitcast.1, bf16[128,4608]{1,0:T(8,128)(2,1)} %hid_ref.1, bf16[128,4608]{1,0:T(8,128)(2,1)} %grad_ref.1, bf16[576,4608]{1,0:T(8,128)(2,1)} %noise_ref.1), custom_call_target="tpu_custom_call" | custom-call | flops 5435817984 | bytes 10616832 | tf_op jit(solution)/shard_map/pallas_call | solution.py:273
  91.9 2.5 %shard_map.60 = (bf16[576,4608]{1,0:T(8,128)(2,1)}, f32[8]{0:T(128)}) custom-call(bf16[576,4608]{1,0:T(8,128)(2,1)S(1)} %get-tuple-element.4.held_ref, f32[8]{0:T(128)S(1)} %get-tuple-element.5.held_norms_ref), custom_call_target="tpu_custom_call" | custom-call | bytes 10616832 | tf_op jit(solution)/shard_map/pallas_call | solution.py:306

commit v4 on v3

--- a/solution.py
+++ b/solution.py
@@ -97,6 +97,10 @@
         def _():
             to(d, k, own_send.at[1], d - CORES).start()
 
+        @pl.when((z == 0) | (z == nz - 1))
+        def _():
+            to(d, k, own_send.at[2], (nz - 1 - z) * CORES + c).start()
+
         to(d, k, mate_send.at[z], mate).start()
 
     repeat(0, EARLY, send_own)
@@ -169,7 +173,7 @@
                 j = far * CORES + c
                 to(j, k, mate_send.at[far], mate).wait_recv()
 
-                @pl.when((ahead >= 0) & (ahead < nz))
+                @pl.when((ahead >= 0) & (ahead < nz) & (h + 1 < nz - 1))
                 def _():
                     to(j, k, fwd_send.at[far], ahead * CORES + c).start()
 
@@ -185,7 +189,7 @@
 
     if share > 1:
         others(nt, t, lambda m: share_copy(m, t).start())
-    repeat(nk, nk * (nz - 2), lambda i: forward(1 + lax.div(i, nk), lax.rem(i, nk)))
+    repeat(nk, nk * (nz - 3), lambda i: forward(1 + lax.div(i, nk), lax.rem(i, nk)))
     if share > 1:
         others(nt, t, lambda m: share_copy(m, m).wait_recv())
     others(ndp, d, lambda j: sqd_copy(j, j).wait_recv())
@@ -229,6 +233,7 @@
     def last(k):
         @pl.when(k < nk)
         def _():
+            forward(nz - 2, k)
             forward(nz - 1, k)
 
         @pl.when(k > 0)
@@ -242,11 +247,19 @@
         def _():
             sent(far, mate_send.at[far])
 
-        @pl.when((z > 0) & (z < nz - 1) & (far != z))
+        @pl.when((far > z) & (z > 0) & (far - z + 1 < nz - 1))
         def _():
             sent(far, fwd_send.at[far])
 
+        @pl.when((far < z) & (z < nz - 1) & (z - far + 1 < nz - 1))
+        def _():
+            sent(far, fwd_send.at[far])
+
     repeat(0, nz, sent_on)
+
+    @pl.when((z == 0) | (z == nz - 1))
+    def _():
+        sent(z, own_send.at[2])
 
 
 def place(pieces, held_ref, held_norms_ref, out_ref, norms_ref, sem):
@@ -287,7 +300,7 @@
             pltpu.VMEM((rows, ndp * SEQ), jnp.bfloat16),
             pltpu.VMEM((nt, NSEG, SEQ), jnp.float32),
             pltpu.VMEM((ndp, NSEG, SEQ), jnp.float32),
-            dma((3,)), dma((nk,)), dma((2,)), dma((nz,)), dma((nz,)), dma((ndp, nk)), dma((ndp,)), dma((ndp,)),
+            dma((3,)), dma((nk,)), dma((3,)), dma((nz,)), dma((nz,)), dma((ndp, nk)), dma((ndp,)), dma((ndp,)),
             dma((nt,)), dma((nt,)), dma((nt,)), dma((nt,)), dma((ndp,)), dma((ndp,)),
         ],
         compiler_params=pltpu.CompilerParams(

time: 94.5 us -> 97.7 us (1.034); the launches traced: 94.4 us -> 96.2 us
  Pallas kernels: 93.8 us -> 95.5 us
    pallas_call x1, Pallas kernels: 91.3 us -> 93.1 us  [per_device(): pl.pallas_call(functools.partial(kernel, ndp, nt, width, share), out_shap...]
where the time goes in v4:
time: 97.7 us; the launch traced here: 96.2 us
  Pallas kernels  95.5 us (98%)
    pallas_call x1, Pallas kernels, per_device(): pl.pallas_call(functools.partial(kernel, ndp, nt, width, share), out_shap...  93.1 us
    pallas_call x1, Pallas kernels, per_device(): pl.pallas_call(functools.partial(place, pieces), out_shape=(jax.ShapeDtyp...  2.46 us

profile of v4, /device:TPU:1, one launch (start us, length us, event | category | flops | bytes accessed | tf_op | source)
XLA Modules:
  0.0 96.2 jit_solution(6173258515687437345)
XLA Ops:
  0.6 93.1 %shard_map.59 = (bf16[576,4608]{1,0:T(8,128)(2,1)S(1)}, f32[8]{0:T(128)S(1)}) custom-call(s32[8,128]{1,0:T(8,128)} %bitcast.1, bf16[128,4608]{1,0:T(8,128)(2,1)} %hid_ref.1, bf16[128,4608]{1,0:T(8,128)(2,1)} %grad_ref.1, bf16[576,4608]{1,0:T(8,128)(2,1)} %noise_ref.1), custom_call_target="tpu_custom_call" | custom-call | flops 5435817984 | bytes 10616832 | tf_op jit(solution)/shard_map/pallas_call | solution.py:286
  93.7 2.5 %shard_map.60 = (bf16[576,4608]{1,0:T(8,128)(2,1)}, f32[8]{0:T(128)}) custom-call(bf16[576,4608]{1,0:T(8,128)(2,1)S(1)} %get-tuple-element.4.held_ref, f32[8]{0:T(128)S(1)} %get-tuple-element.5.held_norms_ref), custom_call_target="tpu_custom_call" | custom-call | bytes 10616832 | tf_op jit(solution)/shard_map/pallas_call | solution.py:319

commit v5 on v3

--- a/solution.py
+++ b/solution.py
@@ -17,7 +17,6 @@
 EPSILON = 1e-06
 CLIP_FRACTION = 4.2
 MESH = pl.DeviceIdType.MESH
-EARLY = 3
 
 
 def clip_bound():
@@ -32,7 +31,7 @@
     ndp, nt, width, share, ids_in, hid_ref, grad_ref, noise_ref, out_ref, norms_ref,
     ids_ref, hall, g, gt, gt_in, wt, sq_t, sq_d,
     load_sem, hid_load, own_send, fwd_send, mate_send, hid_recv, gt_send, gt_recv,
-    share_send, share_recv, sqt_send, sqt_recv, sqd_send, sqd_recv,
+    share_send, share_recv, sqt_send, sqt_recv, sqd_send, sqd_recv, chain,
 ):
     d = lax.axis_index("dp")
     t = lax.axis_index("tensor")
@@ -75,10 +74,32 @@
     load_g.start()
     load_i.start()
 
+    def tell(sem, **device):
+        pl.semaphore_signal(sem, inc=1, device_id=device, device_id_type=MESH)
+
     barrier = pltpu.get_barrier_semaphore()
-    others(ndp, d, lambda j: pl.semaphore_signal(barrier, inc=1, device_id={"dp": j}, device_id_type=MESH))
-    others(nt, t, lambda m: pl.semaphore_signal(barrier, inc=1, device_id={"tensor": m}, device_id_type=MESH))
-    pl.semaphore_wait(barrier, ndp + nt - 2)
+    tell(barrier, dp=mate)
+
+    @pl.when(z > 0)
+    def _():
+        tell(barrier, dp=d - CORES)
+
+    @pl.when(z + 1 < nz)
+    def _():
+        tell(barrier, dp=d + CORES)
+
+    @pl.when(z == 0)
+    def _():
+        others(nt, t, lambda m: tell(barrier, tensor=m))
+        pl.semaphore_wait(barrier, nt + 1)
+
+    @pl.when((z > 0) & (z + 1 < nz))
+    def _():
+        pl.semaphore_wait(barrier, 3)
+
+    @pl.when(z + 1 == nz)
+    def _():
+        pl.semaphore_wait(barrier, 2)
 
     def chunk(j, k):
         return hall.at[k, rows_of(j, SEQ), :]
@@ -99,7 +120,8 @@
 
         to(d, k, mate_send.at[z], mate).start()
 
-    repeat(0, EARLY, send_own)
+    repeat(0, nk, send_own)
+    load_n.start()
 
     load_g.wait()
 
@@ -116,10 +138,7 @@
             gt_send.at[j], gt_recv.at[src_seq], {"dp": j},
         )
 
-    others(ndp, d, lambda j: gt_copy(j, d).start())
     gt_in[d, pl.ds(pl.multiple_of(piece, 16), part), :] = gt[pl.ds(pl.multiple_of(d * rows + piece, 16), part), :]
-    repeat(EARLY, nk, send_own)
-    load_n.start()
 
     def members(j):
         ids = ids_ref[pl.ds(j, 1), :]
@@ -145,7 +164,28 @@
     def sqt_copy(m, src):
         return remote(sq_t.at[src], sq_t.at[src], sqt_send.at[m], sqt_recv.at[src], {"tensor": m})
 
+    @pl.when(z + 1 < nz)
+    def _():
+        pl.semaphore_wait(chain.at[0], 1)
+
+    @pl.when(z > 0)
+    def _():
+        tell(chain.at[0], dp=d - CORES)
+        pl.semaphore_wait(chain.at[3], 1)
+
+    @pl.when(z == 0)
+    def _():
+        others(nt, t, lambda m: tell(chain.at[1], tensor=m))
+        pl.semaphore_wait(chain.at[1], nt - 1)
+        tell(chain.at[2], dp=mate)
+        pl.semaphore_wait(chain.at[2], 1)
+
+    @pl.when(z + 1 < nz)
+    def _():
+        tell(chain.at[3], dp=d + CORES)
+
     others(nt, t, lambda m: sqt_copy(m, t).start())
+    others(ndp, d, lambda j: gt_copy(j, d).start())
     others(nt, t, lambda m: sqt_copy(m, m).wait_recv())
     total = sq_t[0]
     for m in range(1, nt):
@@ -289,6 +329,7 @@
             pltpu.VMEM((ndp, NSEG, SEQ), jnp.float32),
             dma((3,)), dma((nk,)), dma((2,)), dma((nz,)), dma((nz,)), dma((ndp, nk)), dma((ndp,)), dma((ndp,)),
             dma((nt,)), dma((nt,)), dma((nt,)), dma((nt,)), dma((ndp,)), dma((ndp,)),
+            pltpu.SemaphoreType.REGULAR((4,)),
         ],
         compiler_params=pltpu.CompilerParams(
             collective_id=0, has_side_effects=True, vmem_limit_bytes=32 * 1024 * 1024

time: 94.5 us -> 93 us (0.984)
  Pallas kernels: 93.8 us -> 92.1 us
    pallas_call x1, Pallas kernels: 91.3 us -> 89.7 us  [per_device(): pl.pallas_call(functools.partial(kernel, ndp, nt, width, share), out_shap...]
where the time goes in v5:
time: 93 us; the launch traced here: 92.8 us
  Pallas kernels  92.1 us (99%)
    pallas_call x1, Pallas kernels, per_device(): pl.pallas_call(functools.partial(kernel, ndp, nt, width, share), out_shap...  89.7 us
    pallas_call x1, Pallas kernels, per_device(): pl.pallas_call(functools.partial(place, pieces), out_shape=(jax.ShapeDtyp...  2.46 us

profile of v5, /device:TPU:1, one launch (start us, length us, event | category | flops | bytes accessed | tf_op | source)
XLA Modules:
  0.0 92.8 jit_solution(4776066145577860792)
XLA Ops:
  0.6 89.7 %shard_map.59 = (bf16[576,4608]{1,0:T(8,128)(2,1)S(1)}, f32[8]{0:T(128)S(1)}) custom-call(s32[8,128]{1,0:T(8,128)} %bitcast.1, bf16[128,4608]{1,0:T(8,128)(2,1)} %hid_ref.1, bf16[128,4608]{1,0:T(8,128)(2,1)} %grad_ref.1, bf16[576,4608]{1,0:T(8,128)(2,1)} %noise_ref.1), custom_call_target="tpu_custom_call" | custom-call | flops 5435817984 | bytes 10616832 | tf_op jit(solution)/shard_map/pallas_call | solution.py:313
  90.3 2.5 %shard_map.60 = (bf16[576,4608]{1,0:T(8,128)(2,1)}, f32[8]{0:T(128)}) custom-call(bf16[576,4608]{1,0:T(8,128)(2,1)S(1)} %get-tuple-element.4.held_ref, f32[8]{0:T(128)S(1)} %get-tuple-element.5.held_norms_ref), custom_call_target="tpu_custom_call" | custom-call | bytes 10616832 | tf_op jit(solution)/shard_map/pallas_call | solution.py:347

commit v6 on v5

--- a/solution.py
+++ b/solution.py
@@ -28,8 +28,8 @@
 
 
 def kernel(
-    ndp, nt, width, share, ids_in, hid_ref, grad_ref, noise_ref, out_ref, norms_ref,
-    ids_ref, hall, g, gt, gt_in, wt, sq_t, sq_d,
+    ndp, nt, share, keep, ids_in, hid_ref, grad_ref, noise_ref, out_ref, norms_ref, hall, wt,
+    ids_ref, g, gt, gt_in, sq_t, sq_d,
     load_sem, hid_load, own_send, fwd_send, mate_send, hid_recv, gt_send, gt_recv,
     share_send, share_recv, sqt_send, sqt_recv, sqd_send, sqd_recv, chain,
 ):
@@ -40,7 +40,7 @@
     c = lax.rem(d, CORES)
     mate = d + 1 - 2 * c
     rows, cols = out_ref.shape
-    nk = cols // width
+    nk, _, width = hall.shape
     part = rows // share
 
     def remote(src, dst, send, recv, device):
@@ -262,9 +262,12 @@
 
     def multiply(k):
         repeat(0, nz, lambda far: to(far * CORES + 1 - c, k, mate_send.at[far], mate).wait_recv())
-        at = rows_of(k, width)
-        summed = jnp.dot(wt[...], hall[k], preferred_element_type=jnp.float32)
-        out_ref[:, at] = (summed + out_ref[:, at].astype(jnp.float32)).astype(jnp.bfloat16)
+
+        @pl.when(k < nk - keep)
+        def _():
+            at = rows_of(k, width)
+            summed = jnp.dot(wt[...], hall[k], preferred_element_type=jnp.float32)
+            out_ref[:, at] = (summed + out_ref[:, at].astype(jnp.float32)).astype(jnp.bfloat16)
 
     def last(k):
         @pl.when(k < nk)
@@ -289,14 +292,26 @@
     repeat(0, nz, sent_on)
 
 
-def place(pieces, held_ref, held_norms_ref, out_ref, norms_ref, sem):
-    part = out_ref.shape[0] // pieces
-    copies = [pltpu.make_async_copy(held_norms_ref, norms_ref, sem.at[pieces])]
+def place(keep, pieces, held_ref, held_norms_ref, hall, wt, out_ref, norms_ref, done, sem):
+    rows = out_ref.shape[0]
+    nk, _, width = hall.shape
+    part = rows // pieces
+    ready = (nk - keep) * width
+    copies = []
+
+    def put(src, dst):
+        copies.append(pltpu.make_async_copy(src, dst, sem.at[len(copies)]))
+        copies[-1].start()
+
     for i in range(pieces):
-        at = pl.ds(i * part, part)
-        copies.append(pltpu.make_async_copy(held_ref.at[at, :], out_ref.at[at, :], sem.at[i]))
-    for copy in copies:
-        copy.start()
+        at = (pl.ds(i * part, part), pl.ds(0, ready))
+        put(held_ref.at[at], out_ref.at[at])
+    put(held_norms_ref, norms_ref)
+    for i in range(keep):
+        at = pl.ds(ready + i * width, width)
+        summed = jnp.dot(wt[...], hall[nk - keep + i], preferred_element_type=jnp.float32)
+        done[i] = (summed + held_ref[:, at].astype(jnp.float32)).astype(jnp.bfloat16)
+        put(done.at[i], out_ref.at[:, at])
     for copy in copies:
         copy.wait()
 
@@ -310,21 +325,22 @@
     dma = pltpu.SemaphoreType.DMA
     hbm = pl.BlockSpec(memory_space=pltpu.HBM)
     vmem = pl.BlockSpec(memory_space=pltpu.VMEM)
-    out, norms = pl.pallas_call(
-        functools.partial(kernel, ndp, nt, width, share),
+    keep = min(3, nk // 2)
+    out, norms, hall, wt = pl.pallas_call(
+        functools.partial(kernel, ndp, nt, share, keep),
         out_shape=(
             jax.ShapeDtypeStruct((rows, cols), jnp.bfloat16),
             jax.ShapeDtypeStruct((NSEG,), jnp.float32),
+            pltpu.VMEM((nk, ndp * SEQ, width), jnp.bfloat16),
+            pltpu.VMEM((rows, ndp * SEQ), jnp.bfloat16),
         ),
         in_specs=[hbm] * 4,
-        out_specs=(vmem, vmem),
+        out_specs=(vmem,) * 4,
         scratch_shapes=[
             pltpu.VMEM((ndp, SEQ), jnp.int32),
-            pltpu.VMEM((nk, ndp * SEQ, width), jnp.bfloat16),
             pltpu.VMEM((SEQ, D), jnp.bfloat16),
             pltpu.VMEM((D, SEQ), jnp.bfloat16),
             pltpu.VMEM((ndp, rows, SEQ), jnp.bfloat16),
-            pltpu.VMEM((rows, ndp * SEQ), jnp.bfloat16),
             pltpu.VMEM((nt, NSEG, SEQ), jnp.float32),
             pltpu.VMEM((ndp, NSEG, SEQ), jnp.float32),
             dma((3,)), dma((nk,)), dma((2,)), dma((nz,)), dma((nz,)), dma((ndp, nk)), dma((ndp,)), dma((ndp,)),
@@ -332,7 +348,7 @@
             pltpu.SemaphoreType.REGULAR((4,)),
         ],
         compiler_params=pltpu.CompilerParams(
-            collective_id=0, has_side_effects=True, vmem_limit_bytes=32 * 1024 * 1024
+            collective_id=0, has_side_effects=True, vmem_limit_bytes=24 * 1024 * 1024
         ),
         cost_estimate=pl.CostEstimate(
             flops=2 * ndp * SEQ * rows * cols, bytes_accessed=4 * rows * cols, transcendentals=0
@@ -345,17 +361,17 @@
     )
     pieces = 8 if rows % 128 == 0 else 9
     return pl.pallas_call(
-        functools.partial(place, pieces),
+        functools.partial(place, keep, pieces),
         out_shape=(
             jax.ShapeDtypeStruct((rows, cols), jnp.bfloat16),
             jax.ShapeDtypeStruct((NSEG,), jnp.float32),
         ),
-        in_specs=[pl.BlockSpec(memory_space=pl.ANY)] * 2,
+        in_specs=[vmem] * 4,
         out_specs=(pl.BlockSpec(memory_space=pl.ANY),) * 2,
-        scratch_shapes=[dma((pieces + 1,))],
-        compiler_params=pltpu.CompilerParams(vmem_limit_bytes=1024 * 1024),
-        cost_estimate=pl.CostEstimate(flops=0, bytes_accessed=4 * rows * cols, transcendentals=0),
-    )(out, norms)
+        scratch_shapes=[pltpu.VMEM((keep, rows, width), jnp.bfloat16), dma((pieces + 1 + keep,))],
+        compiler_params=pltpu.CompilerParams(vmem_limit_bytes=8 * 1024 * 1024),
+        cost_estimate=pl.CostEstimate(flops=2 * ndp * SEQ * rows * width * keep, bytes_accessed=4 * rows * cols, transcendentals=0),
+    )(out, norms, hall, wt)
 
 
 def solution(mesh):

time: 93 us -> 92.9 us (level)
  no operation moved by 1% of the time
where the time goes in v6:
time: 92.9 us; the launch traced here: 92.7 us
  Pallas kernels  92 us (99%)
    pallas_call x1, Pallas kernels, per_device(): pl.pallas_call(functools.partial(kernel, ndp, nt, share, keep), out_shape...  89.2 us
    pallas_call x1, Pallas kernels, per_device(): pl.pallas_call(functools.partial(place, keep, pieces), out_shape=(jax.Sha...  2.84 us

profile of v6, /device:TPU:1, one launch (start us, length us, event | category | flops | bytes accessed | tf_op | source)
XLA Modules:
  0.0 92.7 jit_solution(2442968316980293105)
XLA Ops:
  0.6 89.2 %shard_map.59 = (bf16[576,4608]{1,0:T(8,128)(2,1)S(1)}, f32[8]{0:T(128)S(1)}, bf16[18,1024,256]{2,1,0:T(8,128)(2,1)S(1)}, bf16[576,1024]{1,0:T(8,128)(2,1)S(1)}) custom-call(s32[8,128]{1,0:T(8,128)} %bitcast.1, bf16[128,4608]{1,0:T(8,128)(2,1)} %hid_ref.1, bf16[128,4608]{1,0:T(8,128)(2,1)} %grad_ref.1, bf16[576,4608]{1,0:T(8,128)(2,1)} %noise_ref.1), custom_call_target="tpu_custom_call" | custom-call | flops 5435817984 | bytes 10616832 | tf_op jit(solution)/shard_map/pallas_call | solution.py:329
  89.8 2.8 %shard_map.60 = (bf16[576,4608]{1,0:T(8,128)(2,1)}, f32[8]{0:T(128)}) custom-call(bf16[576,4608]{1,0:T(8,128)(2,1)S(1)} %get-tuple-element.6.held_ref, f32[8]{0:T(128)S(1)} %get-tuple-element.7.held_norms_ref, bf16[18,1024,256]{2,1,0:T(8,128)(2,1)S(1)} %get-tuple-element.8.hall, bf16[576,1024]{1,0:T(8,128)(2,1)S(1)} %get-tuple-element.9.wt), custom_call_target="tpu_custom_call" | custom-call | flops 905969664 | bytes 10616832 | tf_op jit(solution)/shard_map/pallas_call | solution.py:363

commit v7 on v5

--- a/solution.py
+++ b/solution.py
@@ -80,26 +80,19 @@
     barrier = pltpu.get_barrier_semaphore()
     tell(barrier, dp=mate)
 
+    @pl.when(z + 1 < nz)
+    def _():
+        tell(barrier, dp=d + CORES)
+
+    @pl.when(z == 0)
+    def _():
+        others(nt, t, lambda m: tell(barrier, tensor=m))
+        pl.semaphore_wait(barrier, nt)
+
     @pl.when(z > 0)
     def _():
-        tell(barrier, dp=d - CORES)
-
-    @pl.when(z + 1 < nz)
-    def _():
-        tell(barrier, dp=d + CORES)
-
-    @pl.when(z == 0)
-    def _():
-        others(nt, t, lambda m: tell(barrier, tensor=m))
-        pl.semaphore_wait(barrier, nt + 1)
-
-    @pl.when((z > 0) & (z + 1 < nz))
-    def _():
-        pl.semaphore_wait(barrier, 3)
-
-    @pl.when(z + 1 == nz)
-    def _():
         pl.semaphore_wait(barrier, 2)
+        tell(chain.at[4], dp=d - CORES)
 
     def chunk(j, k):
         return hall.at[k, rows_of(j, SEQ), :]
@@ -107,20 +100,33 @@
     def to(j, k, send, device):
         return remote(chunk(j, k), chunk(j, k), send, hid_recv.at[j, k], {"dp": device})
 
-    def send_own(k):
+    def send_down(k):
         load_h(k).wait()
 
+        @pl.when(z > 0)
+        def _():
+            to(d, k, own_send.at[1], d - CORES).start()
+
+        to(d, k, mate_send.at[z], mate).start()
+
+    def send_up(k):
         @pl.when(z + 1 < nz)
         def _():
             to(d, k, own_send.at[0], d + CORES).start()
 
-        @pl.when(z > 0)
-        def _():
-            to(d, k, own_send.at[1], d - CORES).start()
-
-        to(d, k, mate_send.at[z], mate).start()
-
-    repeat(0, nk, send_own)
+    def send_both(k):
+        send_down(k)
+        send_up(k)
+
+    early = min(4, nk)
+    repeat(0, early, send_down)
+
+    @pl.when(z + 1 < nz)
+    def _():
+        pl.semaphore_wait(chain.at[4], 1)
+
+    repeat(0, early, send_up)
+    repeat(early, nk, send_both)
     load_n.start()
 
     load_g.wait()
@@ -295,8 +301,8 @@
     for i in range(pieces):
         at = pl.ds(i * part, part)
         copies.append(pltpu.make_async_copy(held_ref.at[at, :], out_ref.at[at, :], sem.at[i]))
-    for copy in copies:
-        copy.start()
+    for i, copy in enumerate(copies):
+        copy.start(priority=i % 2)
     for copy in copies:
         copy.wait()
 
@@ -329,7 +335,7 @@
             pltpu.VMEM((ndp, NSEG, SEQ), jnp.float32),
             dma((3,)), dma((nk,)), dma((2,)), dma((nz,)), dma((nz,)), dma((ndp, nk)), dma((ndp,)), dma((ndp,)),
             dma((nt,)), dma((nt,)), dma((nt,)), dma((nt,)), dma((ndp,)), dma((ndp,)),
-            pltpu.SemaphoreType.REGULAR((4,)),
+            pltpu.SemaphoreType.REGULAR((5,)),
         ],
         compiler_params=pltpu.CompilerParams(
             collective_id=0, has_side_effects=True, vmem_limit_bytes=32 * 1024 * 1024

time: 93 us -> 92.3 us (level)
  no operation moved by 1% of the time
where the time goes in v7:
time: 92.3 us; the launch traced here: 92.2 us
  Pallas kernels  91.5 us (99%)
    pallas_call x1, Pallas kernels, per_device(): pl.pallas_call(functools.partial(kernel, ndp, nt, width, share), out_shap...  89.1 us
    pallas_call x1, Pallas kernels, per_device(): pl.pallas_call(functools.partial(place, pieces), out_shape=(jax.ShapeDtyp...  2.46 us

profile of v7, /device:TPU:1, one launch (start us, length us, event | category | flops | bytes accessed | tf_op | source)
XLA Modules:
  0.0 92.2 jit_solution(10867073888000270757)
XLA Ops:
  0.6 89.1 %shard_map.59 = (bf16[576,4608]{1,0:T(8,128)(2,1)S(1)}, f32[8]{0:T(128)S(1)}) custom-call(s32[8,128]{1,0:T(8,128)} %bitcast.1, bf16[128,4608]{1,0:T(8,128)(2,1)} %hid_ref.1, bf16[128,4608]{1,0:T(8,128)(2,1)} %grad_ref.1, bf16[576,4608]{1,0:T(8,128)(2,1)} %noise_ref.1), custom_call_target="tpu_custom_call" | custom-call | flops 5435817984 | bytes 10616832 | tf_op jit(solution)/shard_map/pallas_call | solution.py:319
  89.7 2.5 %shard_map.60 = (bf16[576,4608]{1,0:T(8,128)(2,1)}, f32[8]{0:T(128)}) custom-call(bf16[576,4608]{1,0:T(8,128)(2,1)S(1)} %get-tuple-element.4.held_ref, f32[8]{0:T(128)S(1)} %get-tuple-element.5.held_norms_ref), custom_call_target="tpu_custom_call" | custom-call | bytes 10616832 | tf_op jit(solution)/shard_map/pallas_call | solution.py:353

commit v8 on v7

--- a/solution.py
+++ b/solution.py
@@ -70,23 +70,27 @@
     load_g = pltpu.make_async_copy(grad_ref, g, load_sem.at[0])
     load_n = pltpu.make_async_copy(noise_ref, out_ref, load_sem.at[1])
     load_i = pltpu.make_async_copy(ids_in, ids_ref, load_sem.at[2])
+
+    def tell(sem, **device):
+        pl.semaphore_signal(sem, inc=1, device_id=device, device_id_type=MESH)
+
+    barrier = pltpu.get_barrier_semaphore()
+    tell(barrier, dp=mate)
+
+    @pl.when(z + 1 < nz)
+    def _():
+        tell(barrier, dp=d + CORES)
+
+    @pl.when(z == 0)
+    def _():
+        others(nt, t, lambda m: tell(barrier, tensor=m))
+
     repeat(0, nk, lambda k: load_h(k).start())
     load_g.start()
     load_i.start()
 
-    def tell(sem, **device):
-        pl.semaphore_signal(sem, inc=1, device_id=device, device_id_type=MESH)
-
-    barrier = pltpu.get_barrier_semaphore()
-    tell(barrier, dp=mate)
-
-    @pl.when(z + 1 < nz)
-    def _():
-        tell(barrier, dp=d + CORES)
-
     @pl.when(z == 0)
     def _():
-        others(nt, t, lambda m: tell(barrier, tensor=m))
         pl.semaphore_wait(barrier, nt)
 
     @pl.when(z > 0)
@@ -100,14 +104,21 @@
     def to(j, k, send, device):
         return remote(chunk(j, k), chunk(j, k), send, hid_recv.at[j, k], {"dp": device})
 
+    def send_first(k):
+        @pl.when(z > 0)
+        def _():
+            remote(
+                hid_ref.at[:, rows_of(k, width)], chunk(d, k), own_send.at[1], hid_recv.at[d, k], {"dp": d - CORES}
+            ).start()
+
+    def send_mate(k):
+        load_h(k).wait()
+        to(d, k, mate_send.at[z], mate).start()
+
     def send_down(k):
-        load_h(k).wait()
-
         @pl.when(z > 0)
         def _():
             to(d, k, own_send.at[1], d - CORES).start()
-
-        to(d, k, mate_send.at[z], mate).start()
 
     def send_up(k):
         @pl.when(z + 1 < nz)
@@ -115,11 +126,13 @@
             to(d, k, own_send.at[0], d + CORES).start()
 
     def send_both(k):
+        send_mate(k)
         send_down(k)
         send_up(k)
 
-    early = min(4, nk)
-    repeat(0, early, send_down)
+    early = min(2, nk)
+    repeat(0, early, send_first)
+    repeat(0, early, send_mate)
 
     @pl.when(z + 1 < nz)
     def _():
@@ -301,8 +314,8 @@
     for i in range(pieces):
         at = pl.ds(i * part, part)
         copies.append(pltpu.make_async_copy(held_ref.at[at, :], out_ref.at[at, :], sem.at[i]))
-    for i, copy in enumerate(copies):
-        copy.start(priority=i % 2)
+    for copy in copies:
+        copy.start()
     for copy in copies:
         copy.wait()
 

time: 92.3 us -> 92.3 us (level)
  no operation moved by 1% of the time
where the time goes in v8:
time: 92.3 us; the launch traced here: 92.2 us
  Pallas kernels  91.6 us (99%)
    pallas_call x1, Pallas kernels, per_device(): pl.pallas_call(functools.partial(kernel, ndp, nt, width, share), out_shap...  89.1 us
    pallas_call x1, Pallas kernels, per_device(): pl.pallas_call(functools.partial(place, pieces), out_shape=(jax.ShapeDtyp...  2.46 us

profile of v8, /device:TPU:1, one launch (start us, length us, event | category | flops | bytes accessed | tf_op | source)
XLA Modules:
  0.0 92.2 jit_solution(3649980249106955052)
XLA Ops:
  0.6 89.1 %shard_map.59 = (bf16[576,4608]{1,0:T(8,128)(2,1)S(1)}, f32[8]{0:T(128)S(1)}) custom-call(s32[8,128]{1,0:T(8,128)} %bitcast.1, bf16[128,4608]{1,0:T(8,128)(2,1)} %hid_ref.1, bf16[128,4608]{1,0:T(8,128)(2,1)} %grad_ref.1, bf16[576,4608]{1,0:T(8,128)(2,1)} %noise_ref.1), custom_call_target="tpu_custom_call" | custom-call | flops 5435817984 | bytes 10616832 | tf_op jit(solution)/shard_map/pallas_call | solution.py:332
  89.7 2.5 %shard_map.60 = (bf16[576,4608]{1,0:T(8,128)(2,1)}, f32[8]{0:T(128)}) custom-call(bf16[576,4608]{1,0:T(8,128)(2,1)S(1)} %get-tuple-element.4.held_ref, f32[8]{0:T(128)S(1)} %get-tuple-element.5.held_norms_ref), custom_call_target="tpu_custom_call" | custom-call | bytes 10616832 | tf_op jit(solution)/shard_map/pallas_call | solution.py:366

commit v9 on v8

--- a/solution.py
+++ b/solution.py
@@ -322,7 +322,7 @@
 
 def per_device(ndp, nt, hidden, grad_out, seg_ids, seg_counts, added_noise):
     rows, cols = added_noise.shape
-    width = next(w for w in (256, 384, 128) if cols % w == 0)
+    width = next(w for w in (384, 256, 128) if cols % w == 0)
     share = nt if rows % (16 * nt) == 0 else 1
     nz = ndp // CORES
     nk = cols // width

time: 92.3 us -> 92.2 us (level)
  no operation moved by 1% of the time
where the time goes in v9:
time: 92.2 us; the launch traced here: 92.1 us
  Pallas kernels  91.4 us (99%)
    pallas_call x1, Pallas kernels, per_device(): pl.pallas_call(functools.partial(kernel, ndp, nt, width, share), out_shap...  89 us
    pallas_call x1, Pallas kernels, per_device(): pl.pallas_call(functools.partial(place, pieces), out_shape=(jax.ShapeDtyp...  2.46 us

profile of v9, /device:TPU:1, one launch (start us, length us, event | category | flops | bytes accessed | tf_op | source)
XLA Modules:
  0.0 92.1 jit_solution(10714556077913112696)
XLA Ops:
  0.6 89.0 %shard_map.59 = (bf16[576,4608]{1,0:T(8,128)(2,1)S(1)}, f32[8]{0:T(128)S(1)}) custom-call(s32[8,128]{1,0:T(8,128)} %bitcast.1, bf16[128,4608]{1,0:T(8,128)(2,1)} %hid_ref.1, bf16[128,4608]{1,0:T(8,128)(2,1)} %grad_ref.1, bf16[576,4608]{1,0:T(8,128)(2,1)} %noise_ref.1), custom_call_target="tpu_custom_call" | custom-call | flops 5435817984 | bytes 10616832 | tf_op jit(solution)/shard_map/pallas_call | solution.py:332
  89.6 2.5 %shard_map.60 = (bf16[576,4608]{1,0:T(8,128)(2,1)}, f32[8]{0:T(128)}) custom-call(bf16[576,4608]{1,0:T(8,128)(2,1)S(1)} %get-tuple-element.4.held_ref, f32[8]{0:T(128)S(1)} %get-tuple-element.5.held_norms_ref), custom_call_target="tpu_custom_call" | custom-call | bytes 10616832 | tf_op jit(solution)/shard_map/pallas_call | solution.py:366
